TPU v7x, 32 devices: a whole 2x2x4 slice. The times are simulated.
32 devices in a mesh: section: 2 (over core), expert: 16 (over z, y, x).
Axes of the slice: x: 2, y: 2, z: 4, core: 2. Of those that a mesh axis runs over, the one named last changes fastest.
Arguments:
- tokens: bfloat16 [2, 4096, 1024], P('section', 'expert'), may hold values from -6 to 6
- gates: float32 [2, 4096], P('section', 'expert'), may hold values from 0.2 to 1
- routes: int32 [2, 4096, 1], P('section', 'expert'), may hold values from 0 to 15; in each aligned block of 256 rows (0 to 255, 256 to 511, ..., all dimensions but the last counted through in order) at most 32 rows name the same one
- capacity: int32 [2, 16], P('section', 'expert'), may hold values from 128 to 512
- mem_lengths: int32 [2, 16], P('section', 'expert'), may hold values from 64 to 256
- mem_keys: bfloat16 [2, 2048, 1024], P('section', 'expert')
- mem_values: bfloat16 [2, 2048, 1024], P('section', 'expert'), may hold values from -6 to 6
- q_weight: bfloat16 [2, 1024, 1024], P('section', 'expert'), may hold values from -0.1875 to 0.1875
- out_weight: bfloat16 [2, 1024, 1024], P('section', 'expert'), may hold values from -0.75 to 0.75
- w_in: bfloat16 [2, 16, 1024, 1408], P('section', 'expert'), may hold values from -0.1875 to 0.1875
Outputs:
- expert_hidden: bfloat16 [2, 4096, 1408], P('section', 'expert')
Inputs may be any that keep to these rules, and one draw needn't show every extreme that they name: `routes`: among the 256 rows of one device at most 32 name one expert.
All inputs are finite; a program needn't handle non-finite values.
Results may differ from a plain program's by a relative error of at most 0.013.
Values may be sent and summed in bfloat16 or wider, within the bound.
A program may use at most 64 MiB of HBM per device.

v0:
```python
import jax
import jax.numpy as jnp
from jax import lax
from jax.sharding import PartitionSpec as P

HEADS = 16


def from_behind(x, axis, by):
    peers = lax.axis_size(axis)
    pairs = [(i, i + by) for i in range(peers) if 0 <= i + by < peers]
    return lax.ppermute(x, axis, pairs)


def carried_in(x, axis, combine, identity):
    peers, place = (lax.axis_size(axis), lax.axis_index(axis))
    everything = lax.all_gather(x, axis)
    start = jnp.broadcast_to(jnp.asarray(identity, x.dtype), x.shape)

    def lap(k, before):
        reached = k < place
        new = combine(before, everything[k])
        return jnp.where(reached, new, before)

    return lax.fori_loop(0, peers, lap, start)


def row_folder(left, piece):
    return jnp.dot(left, piece, preferred_element_type=jnp.float32)


def attend_block(query, keys, values, length):
    rows = query.shape[0]
    span = keys.shape[0]
    heads = HEADS
    qh = query.reshape(rows, heads, -1)
    kh = keys.reshape(span, heads, -1)
    vh = values.reshape(span, heads, -1)
    scores = jnp.einsum("qhd,khd->hqk", qh, kh, preferred_element_type=jnp.float32) / jnp.sqrt(
        jnp.float32(qh.shape[2])
    )
    valid = jnp.arange(span, dtype=jnp.int32) < length
    scores = jnp.where(valid[None, None, :], scores, jnp.float32(-1e30))
    scores = scores - jnp.max(scores, axis=-1, keepdims=True)
    weights = jnp.exp(scores)
    probs = (weights / jnp.sum(weights, axis=-1, keepdims=True)).astype(jnp.bfloat16)
    context = jnp.einsum("hqk,khd->qhd", probs, vh, preferred_element_type=jnp.float32)
    return context.reshape(rows, -1).astype(jnp.bfloat16)


def shards(
    tokens, gates, routes, capacity, mem_lengths, mem_keys, mem_values, q_weight, out_weight, w_in
):
    sections = lax.axis_size("section")
    half = sections // 2
    experts = lax.axis_size("expert")
    inputs = tokens[0]
    tok_dev = inputs.shape[0]
    width = inputs.shape[1]
    cap = max(8, 2 * tok_dev // experts)
    remote = from_behind((mem_keys[0], mem_values[0]), "section", half)
    keys = jnp.concatenate([remote[0], mem_keys[0]], axis=0)
    values = jnp.concatenate([remote[1], mem_values[0]], axis=0)
    query = row_folder(inputs, lax.all_gather(q_weight[0], "expert", axis=0, tiled=True)).astype(
        jnp.bfloat16
    )
    context = attend_block(query, keys, values, mem_lengths[0, 0])
    attn_out = row_folder(context, lax.all_gather(out_weight[0], "expert", axis=0, tiled=True))
    decoding = lax.axis_index("section") >= half
    mixed = jnp.where(
        decoding, (inputs.astype(jnp.float32) + attn_out).astype(jnp.bfloat16), inputs
    )
    route = routes[0, :, 0]
    onehot = (route[:, None] == jnp.arange(experts, dtype=jnp.int32)[None, :]).astype(jnp.int32)
    lrank = jnp.sum((jnp.cumsum(onehot, axis=0) - onehot) * onehot, axis=1)
    counts = jnp.sum(onehot, axis=0)
    slot = route * cap + lrank
    placing = (slot[:, None] == jnp.arange(experts * cap, dtype=jnp.int32)[None, :]).astype(
        jnp.bfloat16
    )
    w_local = w_in[0, 0]
    offsets = carried_in(
        counts, "expert", lambda earlier, later: earlier + later, jnp.zeros_like(counts)
    )
    limits = lax.all_gather(capacity[0], "expert", axis=0, tiled=True)
    grank = jnp.sum(onehot * offsets[None, :], axis=1) + lrank
    kept = grank < jnp.sum(onehot * limits[None, :], axis=1)
    sending = jnp.where(kept[:, None], mixed, jnp.zeros_like(mixed))
    buffer = jnp.einsum("ts,td->sd", placing, sending, preferred_element_type=jnp.float32).astype(
        jnp.bfloat16
    )
    received = lax.all_to_all(
        buffer.reshape(experts, cap, width), "expert", split_axis=0, concat_axis=0, tiled=True
    )
    acts = jnp.maximum(
        jnp.dot(
            received.reshape(experts * cap, width), w_local, preferred_element_type=jnp.float32
        ),
        0.0,
    )
    acts = acts.astype(jnp.bfloat16).reshape(experts, cap, -1)
    back = lax.all_to_all(acts, "expert", split_axis=0, concat_axis=0, tiled=True)
    picked = jnp.dot(placing, back.reshape(experts * cap, -1), preferred_element_type=jnp.float32)
    result = (picked * gates[0][:, None]).astype(jnp.bfloat16)
    return result[None, :, :]


def solution(mesh):
    in_specs = (
        P("section", "expert", None),
        P("section", "expert"),
        P("section", "expert", None),
        P("section", "expert"),
        P("section", "expert"),
        P("section", "expert", None),
        P("section", "expert", None),
        P("section", "expert", None),
        P("section", "expert", None),
        P("section", "expert", None, None),
    )
    out_specs = P("section", "expert", None)
    return jax.shard_map(shards, mesh=mesh, in_specs=in_specs, out_specs=out_specs, check_vma=False)
```

profile of v0, /device:TPU:0, one launch (start us, length us, event | category | flops | bytes accessed | tf_op | source)
XLA Modules:
  0.0 218.0 jit_solution(15708951649091174652)
XLA Ops:
  6.5 0.7 all-gather.7.cloned.1.call-update
  7.3 2.5 %collective-permute-start.1 = (bf16[128,1024]{1,0:T(8,128)(2,1)}, bf16[128,1024]{1,0:T(8,128)(2,1)S(1)}, u32[]{:S(2)}, u32[]{:S(2)}) collective-permute-start(bf16[128,1024]{1,0:T(8,128)(2,1)} %bitcast.79), channel_id=1, source_target_pairs={{0,16},{1,17},{2,18},{3,19},{4,20},{5,21},{6,22},{7,23},{8,24},{9,... | collective-permute-start | bytes 786440 | tf_op jit(solution)/shard_map/ppermute | solution.py:12
  9.8 1.3 collective-permute-start
  11.8 0.8 convert_reduce_fusion
  12.6 1.2 dynamic-slice
  15.5 15.6 %all-reduce.2 = (s32[16]{0:T(128)S(1)}, s32[256]{0:T(256)S(1)}) all-reduce(s32[16]{0:T(128)S(1)} %bitcast_dynamic-update-slice_fusion, s32[256]{0:T(256)S(1)} %dynamic-update-slice), channel_id=3, replica_groups=mesh['section'=2,'expert'=16] {'expert'}, use_global_device_ids=true, to_apply=%add.1 | all-reduce | flops 272 | bytes 2176
  32.4 0.7 fusion.49
  33.9 0.8 fusion.48
  35.4 1.8 copy.22
  37.2 1.8 copy.19
  39.0 0.9 copy.21
  39.8 0.8 copy.18
  40.7 33.0 %all-gather.7.cloned.1.call-done = bf16[1,1024,1024]{2,1,0:T(8,128)(2,1)} async-done(((bf16[1,64,1024]{2,1,0:T(8,128)(2,1)}), bf16[1,1024,1024]{2,1,0:T(8,128)(2,1)}) %all-gather.7.cloned.1.call-update) | async-done | bytes 2097168 | tf_op jit(solution)/shard_map/all_gather | solution.py:64
  73.7 3.3 %fusion.17 = bf16[256,1024]{1,0:T(8,128)(2,1)} fusion(bf16[1,1024,1024]{2,1,0:T(8,128)(2,1)} %all-gather.7.cloned.1.call-done, bf16[1,256,1024]{2,1,0:T(8,128)(2,1)} %param.12), kind=kOutput, calls=%fused_computation.23 | convolution fusion | flops 537133056 | bytes 3145728 | tf_op jit(solution)/shard_map/dot_general | solution.py:29
  76.9 1.2 copy.20
  78.2 1.8 fusion.36
  80.0 1.7 fusion.55
  81.7 1.3 fusion.23
  83.0 52.8 %all-gather.9.cloned.1.call-done = bf16[1,1024,1024]{2,1,0:T(8,128)(2,1)} async-done(((bf16[1,64,1024]{2,1,0:T(8,128)(2,1)}), bf16[1,1024,1024]{2,1,0:T(8,128)(2,1)}) %all-gather.9.cloned.1.call-update) | async-done | bytes 2097168 | tf_op jit(solution)/shard_map/all_gather | solution.py:68
  135.8 3.9 %convolution_convert_fusion = bf16[512,1024]{1,0:T(8,128)(2,1)} fusion(bf16[256,1024]{0,1:T(8,128)(2,1)} %bitcast.88, bf16[1,1024,1024]{2,1,0:T(8,128)(2,1)} %all-gather.9.cloned.1.call-done, bf16[1,256,1024]{2,1,0:T(8,128)(2,1)S(1)} %copy-done.3, pred[256]{0:T(512)(128)(4,1)S(1)} %add_compare_fusion, pred[]{:T(512)S(6)} %ge.3, s32[256]{0:T(256)S(1)} %multiply_add_fusion), kind=kOutput, calls=%fused_computation.21 | convolution fusion | flops 807272448 | bytes 4195585 | tf_op jit(solution)/shard_map/ts,td->sd/dot_general | solution.py:89
  139.7 30.1 %all_to_all.10 = bf16[16,32,1024]{2,1,0:T(8,128)(2,1)S(1)} all-to-all(bf16[16,32,1024]{2,1,0:T(8,128)(2,1)} %bitcast.77), channel_id=1, replica_groups=mesh['section'=2,'expert'=16] {'expert'}, dimensions={0} | all-to-all | bytes 2097152 | tf_op jit(solution)/shard_map/all_to_all | solution.py:92
  169.8 1.8 fusion.2
  171.6 38.1 %all_to_all.11 = bf16[16,32,1408]{2,1,0:T(8,128)(2,1)S(1)} all-to-all(bf16[16,32,1408]{2,1,0:T(8,128)(2,1)S(1)} %bitcast.74), channel_id=1, replica_groups=mesh['section'=2,'expert'=16] {'expert'}, dimensions={0} | all-to-all | bytes 2883584 | tf_op jit(solution)/shard_map/all_to_all | solution.py:102
  209.6 1.5 fusion.5
  (45 shorter events, 3.5 us)
Async XLA Ops:
  6.5 163.2 %copy-start = (bf16[1,1,1024,1408]{3,2,1,0:T(8,128)(2,1)S(1)}, bf16[1,1,1024,1408]{3,2,1,0:T(8,128)(2,1)}, u32[]{:S(2)}) copy-start(bf16[1,1,1024,1408]{3,2,1,0:T(8,128)(2,1)} %param.21) | copy-start | bytes 8650756
  6.5 67.1 %all-gather.7.cloned.1.call-start = ((), (), s32[]{:S(2)}) async-start(), calls=%async_computation.2 | async-start | bytes 2228224 | tf_op jit(solution)/shard_map/all_gather | solution.py:64
  7.3 128.6 %all-gather.9.cloned.1.call-start = ((), (), s32[]{:S(2)}) async-start(), calls=%async_computation.3 | async-start | bytes 2228224 | tf_op jit(solution)/shard_map/all_gather | solution.py:68
  7.3 31.7 %collective-permute-start.1 = (bf16[128,1024]{1,0:T(8,128)(2,1)}, bf16[128,1024]{1,0:T(8,128)(2,1)S(1)}, u32[]{:S(2)}, u32[]{:S(2)}) collective-permute-start(bf16[128,1024]{1,0:T(8,128)(2,1)} %bitcast.79), channel_id=1, source_target_pairs={{0,16},{1,17},{2,18},{3,19},{4,20},{5,21},{6,22},{7,23},{8,24},{9,... | collective-permute-start | bytes 786440 | tf_op jit(solution)/shard_map/ppermute | solution.py:12
  9.8 30.0 %collective-permute-start = (bf16[128,1024]{1,0:T(8,128)(2,1)}, bf16[128,1024]{1,0:T(8,128)(2,1)S(1)}, u32[]{:S(2)}, u32[]{:S(2)}) collective-permute-start(bf16[128,1024]{1,0:T(8,128)(2,1)} %bitcast.80), channel_id=1, source_target_pairs={{0,16},{1,17},{2,18},{3,19},{4,20},{5,21},{6,22},{7,23},{8,24},{9,... | collective-permute-start | bytes 786440 | tf_op jit(solution)/shard_map/ppermute | solution.py:12
  80.0 1.8 copy-start.1
  80.0 1.7 copy-start.2
  81.7 54.1 %copy-start.3 = (bf16[1,256,1024]{2,1,0:T(8,128)(2,1)S(1)}, bf16[1,256,1024]{2,1,0:T(8,128)(2,1)}, u32[]{:S(2)}) copy-start(bf16[1,256,1024]{2,1,0:T(8,128)(2,1)} %param.12) | copy-start | bytes 1572868
  171.6 38.1 %copy-start.4 = (f32[1,256]{1,0:T(1,128)S(1)}, f32[1,256]{1,0:T(1,128)}, u32[]{:S(2)}) copy-start(f32[1,256]{1,0:T(1,128)} %param.13) | copy-start | bytes 3076
Sparse Core Ops, SparseCore 0:
  10.1 63.4 all-gather.6
  76.4 59.3 all-gather.8
where the time goes:
time: 219 us; the launch traced here: 218 us
  waiting for transfers between devices  86.5 us (39%)
  blocking collectives  83.7 us (38%)
  between operations  15.5 us (7%)
  matrix products  13.5 us (6%)
  local copies, waits for them, and re-layouts  8.97 us (4%)
  other arithmetic  5.57 us (3%)
  starting transfers between devices  3.85 us (2%)
    all_gather x1, waiting for transfers between devices, shards(): lax.all_gather(out_weight[0], 'expert', axis=0, tiled=True)  52.8 us
    all_to_all x1, blocking collectives, shards(): lax.all_to_all(acts, 'expert', split_axis=0, concat_axis=0, tiled=True)  38.1 us
    all_gather x1, waiting for transfers between devices, shards(): lax.all_gather(q_weight[0], 'expert', axis=0, tiled=True)  33 us
    all_to_all x1, blocking collectives, shards(): lax.all_to_all(buffer.reshape(experts, cap, width), 'expert', split_axis=...  30.1 us
    unnamed x1, blocking collectives  15.6 us
    unnamed x16, local copies, waits for them, and re-layouts  5.75 us
  transfers between devices with their start and end apart: 4, of which 2 were waited for; matrix products, arithmetic and copies ran while one was open for 10% of the time, Pallas kernels for 0%

commit v1 on v0

v1 whole, which is shorter than its diff:
```python
import functools

import jax
import jax.numpy as jnp
from jax import lax
from jax.experimental import pallas as pl
from jax.experimental.pallas import tpu as pltpu
from jax.sharding import PartitionSpec as P

HEADS = 16
LANES = 128
PLANE = 4
MESH = pl.DeviceIdType.MESH
F32 = jnp.float32
BF16 = jnp.bfloat16


def relay(
    sections, experts, cap,
    tokens, gates, routes, capacity, lengths, mem_k, mem_v, q_in, o_in, w_hbm,
    out,
    w_vmem, wbuf, kbuf, vbuf, qbuf, cbuf, mixed, buf, recv, acts, back, acc, cnt,
    local_sem, kv_send, kv_recv, w_send, w_recv,
    cnt_send, cnt_recv, fwd_send, fwd_recv, ret_send, ret_recv,
):
    half = sections // 2
    planes = experts // PLANE
    tok = tokens.shape[1]
    width = tokens.shape[2]
    span = mem_k.shape[1]
    shard = q_in.shape[1]
    rows = PLANE * cap
    sec = lax.axis_index("section")
    me = lax.axis_index("expert")
    a, j = me // PLANE, me % PLANE
    jy, jx = j // 2, j % 2
    by_x = jy * 2 + (1 - jx)
    by_y = (1 - jy) * 2 + jx
    decoding = sec >= half
    pair = lax.rem(sec + half, sections)

    def remote(src, dst, send, recv_sem, section, peer):
        return pltpu.make_async_remote_copy(
            src_ref=src, dst_ref=dst, send_sem=send, recv_sem=recv_sem,
            device_id=(section, peer), device_id_type=MESH,
        )

    get_w = pltpu.make_async_copy(w_hbm.at[0, 0], w_vmem, local_sem.at[0])
    get_w.start()
    own_rows = pl.ds(me * shard, shard)
    own = [
        pltpu.make_async_copy(q_in.at[0], wbuf.at[0, own_rows], local_sem.at[1]),
        pltpu.make_async_copy(o_in.at[0], wbuf.at[1, own_rows], local_sem.at[2]),
        pltpu.make_async_copy(mem_k.at[0], kbuf.at[pl.ds(span, span)], local_sem.at[3]),
        pltpu.make_async_copy(mem_v.at[0], vbuf.at[pl.ds(span, span)], local_sem.at[4]),
    ]

    @pl.when(decoding)
    def _():
        for copy in own:
            copy.start()

    barrier = pltpu.get_barrier_semaphore()

    def greet(k, carry):
        pl.semaphore_signal(
            barrier, inc=1, device_id=(sec, lax.rem(me + k, experts)), device_id_type=MESH
        )
        return carry

    lax.fori_loop(1, experts, greet, 0)
    pl.semaphore_signal(barrier, inc=1, device_id=(pair, me), device_id_type=MESH)
    pl.semaphore_wait(barrier, experts)

    kv = [
        remote(mem_k.at[0], kbuf.at[pl.ds(0, span)], kv_send.at[0], kv_recv.at[0], pair, me),
        remote(mem_v.at[0], vbuf.at[pl.ds(0, span)], kv_send.at[1], kv_recv.at[1], pair, me),
    ]
    first = (by_x, by_y)
    second = (by_y, by_x)

    def w_copy(kind, hop, plane, owner, peer, from_input=False):
        span_ = pl.ds(owner * shard, shard)
        src = (q_in, o_in)[kind].at[0] if from_input else wbuf.at[kind, span_]
        return remote(
            src, wbuf.at[kind, span_], w_send.at[kind, hop, plane], w_recv.at[kind, owner], sec, peer
        )

    @pl.when(jnp.logical_not(decoding))
    def _():
        for copy in kv:
            copy.start()

    @pl.when(decoding)
    def _():
        for kind in range(2):
            def to_planes(dz, carry):
                w_copy(kind, 0, dz, me, lax.rem(a + dz, planes) * PLANE + j, True).start()
                return carry

            lax.fori_loop(1, planes, to_planes, 0)
            w_copy(kind, 1, 0, me, a * PLANE + first[kind], True).start()
            w_copy(kind, 2, 0, me, a * PLANE + second[kind], True).start()

    eye = lax.broadcasted_iota(jnp.int32, (tok, tok), 0) == lax.broadcasted_iota(
        jnp.int32, (tok, tok), 1
    )
    earlier = lax.broadcasted_iota(jnp.int32, (tok, tok), 1) < lax.broadcasted_iota(
        jnp.int32, (tok, tok), 0
    )
    lane = lax.broadcasted_iota(jnp.int32, (tok, LANES), 1).astype(F32)
    route_row = routes[...].astype(F32)
    route_col = jnp.sum(jnp.where(eye, route_row, 0.0), axis=1, keepdims=True)
    gate_col = jnp.sum(jnp.where(eye, gates[...], 0.0), axis=1, keepdims=True)
    onehot = jnp.where(lane == route_col, 1.0, 0.0)
    before = jnp.dot(
        jnp.where(earlier, 1.0, 0.0).astype(BF16), onehot.astype(BF16), preferred_element_type=F32
    )
    lrank = jnp.sum(before * onehot, axis=1, keepdims=True)
    slot_col = route_col * cap + lrank
    slot_row = jnp.sum(jnp.where(eye, slot_col, 0.0), axis=0, keepdims=True)
    cnt[me] = jnp.broadcast_to(jnp.sum(onehot, axis=0, keepdims=True), (8, LANES))

    def cnt_copy(k):
        peer = lax.rem(me + k, experts)
        return remote(cnt.at[me], cnt.at[me], cnt_send.at[k], cnt_recv.at[me], sec, peer)

    def cnt_start(k, carry):
        cnt_copy(k).start()
        return carry

    lax.fori_loop(1, experts, cnt_start, 0)

    @pl.when(jnp.logical_not(decoding))
    def _():
        mixed[...] = tokens[0]

    @pl.when(decoding)
    def _():
        def from_planes(dz, carry):
            plane = lax.rem(a - dz + planes, planes)
            owner = plane * PLANE + j
            for kind in range(2):
                w_copy(kind, 0, dz, owner, owner).wait_recv()
                w_copy(kind, 1, dz, owner, a * PLANE + first[kind]).start()
                w_copy(kind, 2, dz, owner, a * PLANE + second[kind]).start()
            return carry

        lax.fori_loop(1, planes, from_planes, 0)

        def pass_on(dz, carry):
            plane = lax.rem(a - dz + planes, planes)
            for kind in range(2):
                owner = plane * PLANE + first[kind]
                w_copy(kind, 1, dz, owner, a * PLANE + first[kind]).wait_recv()
                w_copy(kind, 3, dz, owner, a * PLANE + second[kind]).start()
            return carry

        lax.fori_loop(0, planes, pass_on, 0)

        def arrive(kind):
            def body(dz, carry):
                plane = lax.rem(a - dz + planes, planes)
                for hop, jj in ((2, second[kind]), (3, 3 - j)):
                    w_copy(kind, hop, dz, plane * PLANE + jj, a * PLANE + second[kind]).wait_recv()
                return carry

            lax.fori_loop(0, planes, body, 0)

        own[0].wait()
        arrive(0)
        tile = 256

        @pl.loop(0, width // tile)
        def _(n):
            cols = pl.ds(pl.multiple_of(n * tile, tile), tile)
            qbuf[:, cols] = jnp.dot(
                tokens[0], wbuf[0, :, cols], preferred_element_type=F32
            ).astype(BF16)

        own[2].wait()
        own[3].wait()
        for copy in kv:
            copy.wait_recv()
        head_dim = width // HEADS
        length = lengths[0, 0]
        valid = lax.broadcasted_iota(jnp.int32, (tok, 2 * span), 1) < length
        low = lax.broadcasted_iota(jnp.int32, (tok, 2 * head_dim), 1) < head_dim
        mask_low = jnp.where(low, 1.0, 0.0).astype(BF16)
        mask_high = jnp.where(low, 0.0, 1.0).astype(BF16)
        scale = 1.0 / (head_dim ** 0.5)

        @pl.loop(0, HEADS // 2)
        def _(i):
            cols = pl.ds(pl.multiple_of(i * 2 * head_dim, 2 * head_dim), 2 * head_dim)
            q2, k2, v2 = qbuf[:, cols], kbuf[:, cols], vbuf[:, cols]
            parts = []
            for mask in (mask_low, mask_high):
                scores = lax.dot_general(
                    q2 * mask, k2, (((1,), (1,)), ((), ())), preferred_element_type=F32
                ) * scale
                scores = jnp.where(valid, scores, -1e30)
                scores = scores - jnp.max(scores, axis=-1, keepdims=True)
                weights = jnp.exp(scores)
                probs = (weights / jnp.sum(weights, axis=-1, keepdims=True)).astype(BF16)
                parts.append(jnp.dot(probs, v2, preferred_element_type=F32))
            cbuf[:, cols] = jnp.where(low, parts[0], parts[1]).astype(BF16)

        own[1].wait()
        arrive(1)

        @pl.loop(0, width // tile)
        def _(n):
            cols = pl.ds(pl.multiple_of(n * tile, tile), tile)
            attn = jnp.dot(cbuf[...], wbuf[1, :, cols], preferred_element_type=F32)
            mixed[:, cols] = (tokens[0, :, cols].astype(F32) + attn).astype(BF16)

    def block(index):
        return pl.ds(pl.multiple_of(index * cap, cap), cap)

    def fwd_copy(peer):
        return remote(
            buf.at[block(peer)], recv.at[block(me)], fwd_send.at[peer], fwd_recv.at[me], sec, peer
        )

    def fwd_arrival(src):
        return remote(
            buf.at[block(src)], recv.at[block(src)], fwd_send.at[src], fwd_recv.at[src], sec, src
        )

    def ret_copy(peer):
        return remote(
            acts.at[block(peer)], back.at[block(me)], ret_send.at[peer], ret_recv.at[me], sec, peer
        )

    def ret_arrival(src):
        return remote(
            acts.at[block(src)], back.at[block(src)], ret_send.at[src], ret_recv.at[src], sec, src
        )

    def in_plane(plane, visit):
        for s in range(PLANE):
            peer = plane * PLANE + lax.rem(j + s, PLANE)
            if s > 0:
                visit(peer)
            else:
                @pl.when(plane != a)
                def _():
                    visit(peer)

    def group(plane):
        return pl.ds(pl.multiple_of(plane * rows, rows), rows)

    def dispatch(dz, carry):
        plane = lax.rem(a + dz, planes)
        at = (lax.broadcasted_iota(jnp.int32, (rows, tok), 0) + plane * rows).astype(F32)
        placing = jnp.where(slot_row == at, 1.0, 0.0).astype(BF16)
        buf[group(plane), :] = jnp.dot(placing, mixed[...], preferred_element_type=F32).astype(BF16)
        in_plane(plane, lambda peer: fwd_copy(peer).start())
        return carry

    lax.fori_loop(0, planes, dispatch, 0)
    recv[block(me), :] = buf[block(me), :]

    def cnt_wait(k, carry):
        src = lax.rem(me + k, experts)
        remote(cnt.at[src], cnt.at[src], cnt_send.at[k], cnt_recv.at[src], sec, src).wait_recv()
        return carry

    lax.fori_loop(1, experts, cnt_wait, 0)
    get_w.wait()
    counts = cnt[:, 0, :].astype(BF16)
    limit = capacity[0, 0].astype(F32)

    def expert(dz, carry):
        plane = lax.rem(a - dz + planes, planes)
        in_plane(plane, lambda src: fwd_arrival(src).wait_recv())
        act = jnp.maximum(
            jnp.dot(recv[group(plane), :], w_vmem[...], preferred_element_type=F32), 0.0
        )
        row = lax.broadcasted_iota(jnp.int32, (rows, experts), 0)
        source = lax.broadcasted_iota(jnp.int32, (rows, experts), 1)
        lower = jnp.where(source < plane * PLANE + row // cap, 1.0, 0.0).astype(BF16)
        sums = jnp.dot(lower, counts, preferred_element_type=F32)
        mine = lax.broadcasted_iota(jnp.int32, (rows, LANES), 1) == me
        offset = jnp.sum(jnp.where(mine, sums, 0.0), axis=1, keepdims=True)
        rank = offset + (lax.broadcasted_iota(jnp.int32, (rows, 1), 0) % cap).astype(F32)
        kept = jnp.where(rank < limit, 1.0, 0.0)
        acts[group(plane), :] = (act * kept).astype(BF16)
        in_plane(plane, lambda peer: ret_copy(peer).start())
        return carry

    lax.fori_loop(0, planes, expert, 0)
    back[block(me), :] = acts[block(me), :]
    acc[...] = jnp.zeros_like(acc)

    def combine(dz, carry):
        plane = lax.rem(a - dz + planes, planes)
        in_plane(plane, lambda src: ret_arrival(src).wait_recv())
        at = (lax.broadcasted_iota(jnp.int32, (tok, rows), 1) + plane * rows).astype(F32)
        placing = jnp.where(slot_col == at, 1.0, 0.0).astype(BF16)
        acc[...] += jnp.dot(placing, back[group(plane), :], preferred_element_type=F32)
        return carry

    lax.fori_loop(0, planes, combine, 0)
    out[0] = (acc[...] * gate_col).astype(BF16)

    def sent(k, carry):
        peer = lax.rem(me + k, experts)
        cnt_copy(k).wait_send()
        fwd_copy(peer).wait_send()
        ret_copy(peer).wait_send()
        return carry

    lax.fori_loop(1, experts, sent, 0)

    @pl.when(jnp.logical_not(decoding))
    def _():
        for copy in kv:
            copy.wait_send()

    @pl.when(decoding)
    def _():
        for kind in range(2):
            def w_sent(dz, carry):
                for hop in range(4):
                    def done():
                        w_copy(kind, hop, dz, me, a * PLANE + second[kind]).wait_send()

                    if hop == 0:
                        pl.when(dz > 0)(done)
                    else:
                        done()
                return carry

            lax.fori_loop(0, planes, w_sent, 0)


def shards(
    tokens, gates, routes, capacity, mem_lengths, mem_keys, mem_values, q_weight, out_weight, w_in
):
    sections = lax.axis_size("section")
    experts = lax.axis_size("expert")
    tok, width = tokens.shape[1:]
    hidden = w_in.shape[3]
    span = mem_keys.shape[1]
    cap = max(16, 2 * tok // experts)
    slots = experts * cap
    planes = experts // PLANE
    dma = pltpu.SemaphoreType.DMA
    vmem = pl.BlockSpec(memory_space=pltpu.VMEM)
    smem = pl.BlockSpec(memory_space=pltpu.SMEM)
    hbm = pl.BlockSpec(memory_space=pl.ANY)
    return pl.pallas_call(
        functools.partial(relay, sections, experts, cap),
        out_shape=jax.ShapeDtypeStruct((1, tok, hidden), BF16),
        in_specs=[vmem, vmem, vmem, smem, smem, hbm, hbm, hbm, hbm, hbm],
        out_specs=vmem,
        scratch_shapes=[
            pltpu.VMEM((width, hidden), BF16),
            pltpu.VMEM((2, width, width), BF16),
            pltpu.VMEM((2 * span, width), BF16),
            pltpu.VMEM((2 * span, width), BF16),
            pltpu.VMEM((tok, width), BF16),
            pltpu.VMEM((tok, width), BF16),
            pltpu.VMEM((tok, width), BF16),
            pltpu.VMEM((slots, width), BF16),
            pltpu.VMEM((slots, width), BF16),
            pltpu.VMEM((slots, hidden), BF16),
            pltpu.VMEM((slots, hidden), BF16),
            pltpu.VMEM((tok, hidden), F32),
            pltpu.VMEM((experts, 8, LANES), F32),
            dma((5,)),
            dma((2,)),
            dma((2,)),
            dma((2, 4, planes)),
            dma((2, experts)),
            dma((experts,)),
            dma((experts,)),
            dma((experts,)),
            dma((experts,)),
            dma((experts,)),
            dma((experts,)),
        ],
        compiler_params=pltpu.CompilerParams(
            collective_id=0, has_side_effects=True, vmem_limit_bytes=48 * 1024 * 1024
        ),
        cost_estimate=pl.CostEstimate(
            flops=4 * tok * width * width + 2 * slots * width * hidden,
            bytes_accessed=2 * width * hidden + 8 * width * width,
            transcendentals=HEADS * tok * 2 * span,
        ),
    )(
        tokens, gates, routes.reshape(1, tok), capacity, mem_lengths,
        mem_keys, mem_values, q_weight, out_weight, w_in,
    )


def solution(mesh):
    in_specs = (
        P("section", "expert", None),
        P("section", "expert"),
        P("section", "expert", None),
        P("section", "expert"),
        P("section", "expert"),
        P("section", "expert", None),
        P("section", "expert", None),
        P("section", "expert", None),
        P("section", "expert", None),
        P("section", "expert", None, None),
    )
    out_specs = P("section", "expert", None)
    return jax.shard_map(shards, mesh=mesh, in_specs=in_specs, out_specs=out_specs, check_vma=False)
```

time: 219 us -> 104 us (0.47)
  the two profiles are of different devices: /device:TPU:0 before, /device:TPU:7 now
where the time goes in v1:
time: 104 us; the launch traced here: 102 us
  Pallas kernels  91.9 us (88%)
  local copies, waits for them, and re-layouts  8.77 us (8%)
  between operations  1.32 us (1%)
    pallas_call x1, Pallas kernels, shards(): pl.pallas_call(functools.partial(relay, sections, experts, cap), out_shap...  91.9 us
    unnamed x17, local copies, waits for them, and re-layouts  8.77 us

profile of v1, /device:TPU:7, one launch (start us, length us, event | category | flops | bytes accessed | tf_op | source)
XLA Modules:
  0.0 102.0 jit_solution(13705265995687356407)
XLA Ops:
  1.3 0.0 copy-start
  1.3 1.8 %copy-done = bf16[1,1,1024,1408]{3,2,1,0:T(8,128)(2,1)S(1)} copy-done((bf16[1,1,1024,1408]{3,2,1,0:T(8,128)(2,1)S(1)}, bf16[1,1,1024,1408]{3,2,1,0:T(8,128)(2,1)}, u32[]{:S(2)}) %copy-start) | copy-done | bytes 2883608
  3.1 0.0 copy-start.1
  3.1 1.0 %copy-done.1 = bf16[1,256,1024]{2,1,0:T(8,128)(2,1)S(1)} copy-done((bf16[1,256,1024]{2,1,0:T(8,128)(2,1)S(1)}, bf16[1,256,1024]{2,1,0:T(8,128)(2,1)}, u32[]{:S(2)}) %copy-start.1) | copy-done | bytes 524312
  4.2 0.0 copy-start.2
  4.2 0.9 copy-done.2
  5.1 0.0 copy-start.3
  5.1 0.9 copy-done.3
  6.1 0.0 copy-start.4
  6.1 0.9 copy-done.4
  7.0 0.0 copy-start.5
  7.0 0.9 copy-done.5
  7.9 0.0 copy-start.6
  7.9 0.7 copy-done.6
  8.5 0.0 copy-start.7
  8.5 0.7 copy-done.7
  9.2 91.9 %shard_map.100 = bf16[1,256,1408]{2,1,0:T(8,128)(2,1)S(1)} custom-call(bf16[1,256,1024]{2,1,0:T(8,128)(2,1)S(1)} %copy-done.1, f32[1,256]{1,0:T(1,128)S(1)} %copy-done.6, s32[1,256]{1,0:T(1,128)S(1)} %bitcast.1, s32[1,1]{1,0:T(1,128)S(6)} %copy.12.capacity, s32[1,1]{1,0:T(1,128)S(6)} %copy.13.lengths, bf16[1,128,1024]{2,1,0:T(8,128)(2,1)S(1)} %copy-done.2, ...), custom_call_target="tpu_custom_call" | custom-call | flops 2550136832 | bytes 11272192 | tf_op jit(solution)/shard_map/pallas_call | solution.py:354
  101.2 0.9 copy.14
Async XLA Ops:
  1.3 1.8 %copy-start = (bf16[1,1,1024,1408]{3,2,1,0:T(8,128)(2,1)S(1)}, bf16[1,1,1024,1408]{3,2,1,0:T(8,128)(2,1)}, u32[]{:S(2)}) copy-start(bf16[1,1,1024,1408]{3,2,1,0:T(8,128)(2,1)} %w_hbm.1) | copy-start | bytes 8650756
  3.1 1.0 %copy-start.1 = (bf16[1,256,1024]{2,1,0:T(8,128)(2,1)S(1)}, bf16[1,256,1024]{2,1,0:T(8,128)(2,1)}, u32[]{:S(2)}) copy-start(bf16[1,256,1024]{2,1,0:T(8,128)(2,1)} %tokens.1) | copy-start | bytes 1572868
  4.2 0.9 copy-start.2
  5.1 0.9 copy-start.3
  6.1 0.9 copy-start.4
  7.0 0.9 copy-start.5
  7.9 0.7 copy-start.6
  8.5 0.7 copy-start.7

commit v2 on v1

--- a/solution.py
+++ b/solution.py
@@ -19,8 +19,8 @@
     sections, experts, cap,
     tokens, gates, routes, capacity, lengths, mem_k, mem_v, q_in, o_in, w_hbm,
     out,
-    w_vmem, wbuf, kbuf, vbuf, qbuf, cbuf, mixed, buf, recv, acts, back, acc, cnt,
-    local_sem, kv_send, kv_recv, w_send, w_recv,
+    w_vmem, tok_vmem, wbuf, kbuf, vbuf, qbuf, cbuf, mixed, buf, recv, acts, back, acc, cnt,
+    turn, local_sem, kv_send, kv_recv, w_send, w_recv,
     cnt_send, cnt_recv, fwd_send, fwd_recv, ret_send, ret_recv,
 ):
     half = sections // 2
@@ -47,6 +47,8 @@
 
     get_w = pltpu.make_async_copy(w_hbm.at[0, 0], w_vmem, local_sem.at[0])
     get_w.start()
+    to_mixed = pltpu.make_async_copy(tokens.at[0], mixed, local_sem.at[5])
+    to_vmem = pltpu.make_async_copy(tokens.at[0], tok_vmem, local_sem.at[5])
     own_rows = pl.ds(me * shard, shard)
     own = [
         pltpu.make_async_copy(q_in.at[0], wbuf.at[0, own_rows], local_sem.at[1]),
@@ -55,8 +57,13 @@
         pltpu.make_async_copy(mem_v.at[0], vbuf.at[pl.ds(span, span)], local_sem.at[4]),
     ]
 
+    @pl.when(jnp.logical_not(decoding))
+    def _():
+        to_mixed.start()
+
     @pl.when(decoding)
     def _():
+        to_vmem.start()
         for copy in own:
             copy.start()
 
@@ -76,8 +83,12 @@
         remote(mem_k.at[0], kbuf.at[pl.ds(0, span)], kv_send.at[0], kv_recv.at[0], pair, me),
         remote(mem_v.at[0], vbuf.at[pl.ds(0, span)], kv_send.at[1], kv_recv.at[1], pair, me),
     ]
-    first = (by_x, by_y)
-    second = (by_y, by_x)
+
+    def first(plane):
+        return jnp.where(plane % 2 == 0, by_x, by_y)
+
+    def second(plane):
+        return jnp.where(plane % 2 == 0, by_y, by_x)
 
     def w_copy(kind, hop, plane, owner, peer, from_input=False):
         span_ = pl.ds(owner * shard, shard)
@@ -99,8 +110,8 @@
                 return carry
 
             lax.fori_loop(1, planes, to_planes, 0)
-            w_copy(kind, 1, 0, me, a * PLANE + first[kind], True).start()
-            w_copy(kind, 2, 0, me, a * PLANE + second[kind], True).start()
+            w_copy(kind, 1, 0, me, a * PLANE + first(a), True).start()
+            w_copy(kind, 2, 0, me, a * PLANE + second(a), True).start()
 
     eye = lax.broadcasted_iota(jnp.int32, (tok, tok), 0) == lax.broadcasted_iota(
         jnp.int32, (tok, tok), 1
@@ -133,40 +144,47 @@
 
     @pl.when(jnp.logical_not(decoding))
     def _():
-        mixed[...] = tokens[0]
+        to_mixed.wait()
+        pl.semaphore_wait(turn, 1)
 
     @pl.when(decoding)
     def _():
-        def from_planes(dz, carry):
-            plane = lax.rem(a - dz + planes, planes)
-            owner = plane * PLANE + j
-            for kind in range(2):
+        def from_planes(kind):
+            def body(dz, carry):
+                plane = lax.rem(a - dz + planes, planes)
+                owner = plane * PLANE + j
                 w_copy(kind, 0, dz, owner, owner).wait_recv()
-                w_copy(kind, 1, dz, owner, a * PLANE + first[kind]).start()
-                w_copy(kind, 2, dz, owner, a * PLANE + second[kind]).start()
-            return carry
-
-        lax.fori_loop(1, planes, from_planes, 0)
-
-        def pass_on(dz, carry):
-            plane = lax.rem(a - dz + planes, planes)
-            for kind in range(2):
-                owner = plane * PLANE + first[kind]
-                w_copy(kind, 1, dz, owner, a * PLANE + first[kind]).wait_recv()
-                w_copy(kind, 3, dz, owner, a * PLANE + second[kind]).start()
-            return carry
-
-        lax.fori_loop(0, planes, pass_on, 0)
+                w_copy(kind, 1, dz, owner, a * PLANE + first(plane)).start()
+                w_copy(kind, 2, dz, owner, a * PLANE + second(plane)).start()
+                return carry
+
+            lax.fori_loop(1, planes, body, 0)
+
+        def pass_on(kind):
+            def body(dz, carry):
+                plane = lax.rem(a - dz + planes, planes)
+                owner = plane * PLANE + first(plane)
+                w_copy(kind, 1, dz, owner, a * PLANE + first(plane)).wait_recv()
+                w_copy(kind, 3, dz, owner, a * PLANE + second(plane)).start()
+                return carry
+
+            lax.fori_loop(0, planes, body, 0)
 
         def arrive(kind):
             def body(dz, carry):
                 plane = lax.rem(a - dz + planes, planes)
-                for hop, jj in ((2, second[kind]), (3, 3 - j)):
-                    w_copy(kind, hop, dz, plane * PLANE + jj, a * PLANE + second[kind]).wait_recv()
+                for hop, jj in ((2, second(plane)), (3, 3 - j)):
+                    w_copy(kind, hop, dz, plane * PLANE + jj, a * PLANE + second(plane)).wait_recv()
                 return carry
 
             lax.fori_loop(0, planes, body, 0)
 
+        from_planes(0)
+        pass_on(0)
+        from_planes(1)
+        pl.semaphore_signal(turn, inc=1, device_id=(pair, me), device_id_type=MESH)
+        pass_on(1)
+        to_vmem.wait()
         own[0].wait()
         arrive(0)
         tile = 256
@@ -175,7 +193,7 @@
         def _(n):
             cols = pl.ds(pl.multiple_of(n * tile, tile), tile)
             qbuf[:, cols] = jnp.dot(
-                tokens[0], wbuf[0, :, cols], preferred_element_type=F32
+                tok_vmem[...], wbuf[0, :, cols], preferred_element_type=F32
             ).astype(BF16)
 
         own[2].wait()
@@ -213,7 +231,7 @@
         def _(n):
             cols = pl.ds(pl.multiple_of(n * tile, tile), tile)
             attn = jnp.dot(cbuf[...], wbuf[1, :, cols], preferred_element_type=F32)
-            mixed[:, cols] = (tokens[0, :, cols].astype(F32) + attn).astype(BF16)
+            mixed[:, cols] = (tok_vmem[:, cols].astype(F32) + attn).astype(BF16)
 
     def block(index):
         return pl.ds(pl.multiple_of(index * cap, cap), cap)
@@ -325,7 +343,7 @@
             def w_sent(dz, carry):
                 for hop in range(4):
                     def done():
-                        w_copy(kind, hop, dz, me, a * PLANE + second[kind]).wait_send()
+                        w_copy(kind, hop, dz, me, a * PLANE + by_x).wait_send()
 
                     if hop == 0:
                         pl.when(dz > 0)(done)
@@ -354,10 +372,11 @@
     return pl.pallas_call(
         functools.partial(relay, sections, experts, cap),
         out_shape=jax.ShapeDtypeStruct((1, tok, hidden), BF16),
-        in_specs=[vmem, vmem, vmem, smem, smem, hbm, hbm, hbm, hbm, hbm],
+        in_specs=[hbm, vmem, vmem, smem, smem, hbm, hbm, hbm, hbm, hbm],
         out_specs=vmem,
         scratch_shapes=[
             pltpu.VMEM((width, hidden), BF16),
+            pltpu.VMEM((tok, width), BF16),
             pltpu.VMEM((2, width, width), BF16),
             pltpu.VMEM((2 * span, width), BF16),
             pltpu.VMEM((2 * span, width), BF16),
@@ -370,7 +389,8 @@
             pltpu.VMEM((slots, hidden), BF16),
             pltpu.VMEM((tok, hidden), F32),
             pltpu.VMEM((experts, 8, LANES), F32),
-            dma((5,)),
+            pltpu.SemaphoreType.REGULAR,
+            dma((6,)),
             dma((2,)),
             dma((2,)),
             dma((2, 4, planes)),
@@ -383,7 +403,7 @@
             dma((experts,)),
         ],
         compiler_params=pltpu.CompilerParams(
-            collective_id=0, has_side_effects=True, vmem_limit_bytes=48 * 1024 * 1024
+            collective_id=0, has_side_effects=True, vmem_limit_bytes=63 * 1024 * 1024
         ),
         cost_estimate=pl.CostEstimate(
             flops=4 * tok * width * width + 2 * slots * width * hidden,

time: 104 us -> 89.6 us (0.86); the launches traced: 102 us -> 89.4 us
  local copies, waits for them, and re-layouts: 8.77 us -> 2.02 us
  Pallas kernels: 91.9 us -> 86 us
    unnamed x17 -> x1, local copies, waits for them, and re-layouts: 8.77 us -> 2.02 us
    pallas_call x1, Pallas kernels: 91.9 us -> 86 us  [shards(): pl.pallas_call(functools.partial(relay, sections, experts, cap), out_shap...]
where the time goes in v2:
time: 89.6 us; the launch traced here: 89.4 us
  Pallas kernels  86 us (96%)
  local copies, waits for them, and re-layouts  2.02 us (2%)
  between operations  1.3 us (1%)
    pallas_call x1, Pallas kernels, shards(): pl.pallas_call(functools.partial(relay, sections, experts, cap), out_shap...  86 us
    unnamed x1, local copies, waits for them, and re-layouts  2.02 us

profile of v2, /device:TPU:7, one launch (start us, length us, event | category | flops | bytes accessed | tf_op | source)
XLA Modules:
  0.0 89.4 jit_solution(4906344177004101318)
XLA Ops:
  1.3 86.0 %shard_map.100 = bf16[1,256,1408]{2,1,0:T(8,128)(2,1)} custom-call(bf16[1,256,1024]{2,1,0:T(8,128)(2,1)} %tokens.1, f32[1,256]{1,0:T(1,128)} %gates.1, s32[1,256]{1,0:T(1,128)} %bitcast.1, s32[1,1]{1,0:T(1,128)S(6)} %copy.12.capacity, s32[1,1]{1,0:T(1,128)S(6)} %copy.13.lengths, bf16[1,128,1024]{2,1,0:T(8,128)(2,1)} %mem_k.1, bf16[1,128,1024]{2,1,0:T(8,128)(2,1)} %mem_v.1, ...), custom_call_target="tpu_custom_call" | custom-call | flops 2550136832 | bytes 11272192 | tf_op jit(solution)/shard_map/pallas_call | solution.py:372
  87.4 2.0 %copy.14 = bf16[1,256,1408]{2,1,0:T(8,128)(2,1)} copy(bf16[1,256,1408]{2,1,0:T(8,128)(2,1)} %shard_map.100) | data formatting | bytes 1441792

commit v3 on v2

--- a/solution.py
+++ b/solution.py
@@ -266,11 +266,19 @@
                 def _():
                     visit(peer)
 
+    mid = max(planes // 2, 1)
+    side = a // mid
+
+    def visit_order(t):
+        across = jnp.where(t < planes - mid, 1, 0)
+        base = lax.rem(side + across, planes // mid) * mid
+        return base + lax.rem(a + t + 1 - across, mid)
+
     def group(plane):
         return pl.ds(pl.multiple_of(plane * rows, rows), rows)
 
     def dispatch(dz, carry):
-        plane = lax.rem(a + dz, planes)
+        plane = visit_order(dz)
         at = (lax.broadcasted_iota(jnp.int32, (rows, tok), 0) + plane * rows).astype(F32)
         placing = jnp.where(slot_row == at, 1.0, 0.0).astype(BF16)
         buf[group(plane), :] = jnp.dot(placing, mixed[...], preferred_element_type=F32).astype(BF16)
@@ -291,7 +299,7 @@
     limit = capacity[0, 0].astype(F32)
 
     def expert(dz, carry):
-        plane = lax.rem(a - dz + planes, planes)
+        plane = visit_order(dz)
         in_plane(plane, lambda src: fwd_arrival(src).wait_recv())
         act = jnp.maximum(
             jnp.dot(recv[group(plane), :], w_vmem[...], preferred_element_type=F32), 0.0
@@ -313,7 +321,7 @@
     acc[...] = jnp.zeros_like(acc)
 
     def combine(dz, carry):
-        plane = lax.rem(a - dz + planes, planes)
+        plane = visit_order(dz)
         in_plane(plane, lambda src: ret_arrival(src).wait_recv())
         at = (lax.broadcasted_iota(jnp.int32, (tok, rows), 1) + plane * rows).astype(F32)
         placing = jnp.where(slot_col == at, 1.0, 0.0).astype(BF16)

time: 89.6 us -> 83 us (0.926); the launches traced: 89.4 us -> 81.4 us
  Pallas kernels: 86 us -> 78.1 us
    pallas_call x1, Pallas kernels: 86 us -> 78.1 us  [shards(): pl.pallas_call(functools.partial(relay, sections, experts, cap), out_shap...]
where the time goes in v3:
time: 83 us; the launch traced here: 81.4 us
  Pallas kernels  78.1 us (94%)
  local copies, waits for them, and re-layouts  2.02 us (2%)
  between operations  1.3 us (2%)
    pallas_call x1, Pallas kernels, shards(): pl.pallas_call(functools.partial(relay, sections, experts, cap), out_shap...  78.1 us
    unnamed x1, local copies, waits for them, and re-layouts  2.02 us

profile of v3, /device:TPU:7, one launch (start us, length us, event | category | flops | bytes accessed | tf_op | source)
XLA Modules:
  0.0 81.4 jit_solution(17783235322692258870)
XLA Ops:
  1.3 78.1 %shard_map.100 = bf16[1,256,1408]{2,1,0:T(8,128)(2,1)} custom-call(bf16[1,256,1024]{2,1,0:T(8,128)(2,1)} %tokens.1, f32[1,256]{1,0:T(1,128)} %gates.1, s32[1,256]{1,0:T(1,128)} %bitcast.1, s32[1,1]{1,0:T(1,128)S(6)} %copy.12.capacity, s32[1,1]{1,0:T(1,128)S(6)} %copy.13.lengths, bf16[1,128,1024]{2,1,0:T(8,128)(2,1)} %mem_k.1, bf16[1,128,1024]{2,1,0:T(8,128)(2,1)} %mem_v.1, ...), custom_call_target="tpu_custom_call" | custom-call | flops 2550136832 | bytes 11272192 | tf_op jit(solution)/shard_map/pallas_call | solution.py:380
  79.4 2.0 %copy.14 = bf16[1,256,1408]{2,1,0:T(8,128)(2,1)} copy(bf16[1,256,1408]{2,1,0:T(8,128)(2,1)} %shard_map.100) | data formatting | bytes 1441792

commit v4 on v3

--- a/solution.py
+++ b/solution.py
@@ -105,13 +105,16 @@
     @pl.when(decoding)
     def _():
         for kind in range(2):
-            def to_planes(dz, carry):
-                w_copy(kind, 0, dz, me, lax.rem(a + dz, planes) * PLANE + j, True).start()
-                return carry
-
-            lax.fori_loop(1, planes, to_planes, 0)
-            w_copy(kind, 1, 0, me, a * PLANE + first(a), True).start()
-            w_copy(kind, 2, 0, me, a * PLANE + second(a), True).start()
+            @pl.when(a + 1 < planes)
+            def _():
+                w_copy(kind, 0, a, me, me + PLANE, True).start()
+
+            @pl.when(a >= 1)
+            def _():
+                w_copy(kind, 4, a, me, me - PLANE, True).start()
+
+            w_copy(kind, 1, a, me, a * PLANE + first(a), True).start()
+            w_copy(kind, 2, a, me, a * PLANE + second(a), True).start()
 
     eye = lax.broadcasted_iota(jnp.int32, (tok, tok), 0) == lax.broadcasted_iota(
         jnp.int32, (tok, tok), 1
@@ -149,26 +152,41 @@
 
     @pl.when(decoding)
     def _():
+        def nearest(visit):
+            def body(dz, carry):
+                for step in (-1, 1):
+                    plane = a + step * dz
+
+                    @pl.when(jnp.logical_and(plane >= 0, plane < planes))
+                    def _():
+                        visit(plane, a - step)
+
+                return carry
+
+            lax.fori_loop(1, planes, body, 0)
+
         def from_planes(kind):
-            def body(dz, carry):
-                plane = lax.rem(a - dz + planes, planes)
+            def visit(plane, onward):
                 owner = plane * PLANE + j
-                w_copy(kind, 0, dz, owner, owner).wait_recv()
-                w_copy(kind, 1, dz, owner, a * PLANE + first(plane)).start()
-                w_copy(kind, 2, dz, owner, a * PLANE + second(plane)).start()
-                return carry
-
-            lax.fori_loop(1, planes, body, 0)
+                w_copy(kind, 0, plane, owner, owner).wait_recv()
+
+                @pl.when(jnp.logical_and(onward >= 0, onward < planes))
+                def _():
+                    w_copy(kind, 0, plane, owner, onward * PLANE + j).start()
+
+                w_copy(kind, 1, plane, owner, a * PLANE + first(plane)).start()
+                w_copy(kind, 2, plane, owner, a * PLANE + second(plane)).start()
+
+            nearest(visit)
 
         def pass_on(kind):
-            def body(dz, carry):
-                plane = lax.rem(a - dz + planes, planes)
+            def visit(plane, onward):
                 owner = plane * PLANE + first(plane)
-                w_copy(kind, 1, dz, owner, a * PLANE + first(plane)).wait_recv()
-                w_copy(kind, 3, dz, owner, a * PLANE + second(plane)).start()
-                return carry
-
-            lax.fori_loop(0, planes, body, 0)
+                w_copy(kind, 1, plane, owner, a * PLANE + first(plane)).wait_recv()
+                w_copy(kind, 3, plane, owner, a * PLANE + second(plane)).start()
+
+            visit(a, a)
+            nearest(visit)
 
         def arrive(kind):
             def body(dz, carry):
@@ -348,18 +366,28 @@
     @pl.when(decoding)
     def _():
         for kind in range(2):
-            def w_sent(dz, carry):
-                for hop in range(4):
-                    def done():
-                        w_copy(kind, hop, dz, me, a * PLANE + by_x).wait_send()
-
-                    if hop == 0:
-                        pl.when(dz > 0)(done)
-                    else:
-                        done()
+            def w_sent(plane, carry):
+                def left(hop):
+                    w_copy(kind, hop, plane, me, a * PLANE + by_x).wait_send()
+
+                for hop in (1, 2, 3):
+                    left(hop)
+                upward = plane <= a
+
+                @pl.when(jnp.logical_or(
+                    jnp.logical_and(upward, a + 1 < planes),
+                    jnp.logical_and(jnp.logical_not(upward), a >= 1),
+                ))
+                def _():
+                    left(0)
+
                 return carry
 
             lax.fori_loop(0, planes, w_sent, 0)
+
+            @pl.when(a >= 1)
+            def _():
+                w_copy(kind, 4, a, me, me - PLANE).wait_send()
 
 
 def shards(
@@ -401,7 +429,7 @@
             dma((6,)),
             dma((2,)),
             dma((2,)),
-            dma((2, 4, planes)),
+            dma((2, 5, planes)),
             dma((2, experts)),
             dma((experts,)),
             dma((experts,)),

time: 83 us -> 84.5 us (1.018)
  the two profiles are of different devices: /device:TPU:7 before, /device:TPU:11 now
where the time goes in v4:
time: 84.5 us; the launch traced here: 84.3 us
  Pallas kernels  81 us (96%)
  local copies, waits for them, and re-layouts  2.02 us (2%)
  between operations  1.3 us (2%)
    pallas_call x1, Pallas kernels, shards(): pl.pallas_call(functools.partial(relay, sections, experts, cap), out_shap...  81 us
    unnamed x1, local copies, waits for them, and re-layouts  2.02 us

profile of v4, /device:TPU:11, one launch (start us, length us, event | category | flops | bytes accessed | tf_op | source)
XLA Modules:
  0.0 84.3 jit_solution(1461243465284529494)
XLA Ops:
  1.3 81.0 %shard_map.100 = bf16[1,256,1408]{2,1,0:T(8,128)(2,1)} custom-call(bf16[1,256,1024]{2,1,0:T(8,128)(2,1)} %tokens.1, f32[1,256]{1,0:T(1,128)} %gates.1, s32[1,256]{1,0:T(1,128)} %bitcast.1, s32[1,1]{1,0:T(1,128)S(6)} %copy.12.capacity, s32[1,1]{1,0:T(1,128)S(6)} %copy.13.lengths, bf16[1,128,1024]{2,1,0:T(8,128)(2,1)} %mem_k.1, bf16[1,128,1024]{2,1,0:T(8,128)(2,1)} %mem_v.1, ...), custom_call_target="tpu_custom_call" | custom-call | flops 2550136832 | bytes 11272192 | tf_op jit(solution)/shard_map/pallas_call | solution.py:408
  82.3 2.0 %copy.14 = bf16[1,256,1408]{2,1,0:T(8,128)(2,1)} copy(bf16[1,256,1408]{2,1,0:T(8,128)(2,1)} %shard_map.100) | data formatting | bytes 1441792

commit v5 on v3

--- a/solution.py
+++ b/solution.py
@@ -180,9 +180,9 @@
             lax.fori_loop(0, planes, body, 0)
 
         from_planes(0)
+        pl.semaphore_signal(turn, inc=1, device_id=(pair, me), device_id_type=MESH)
         pass_on(0)
         from_planes(1)
-        pl.semaphore_signal(turn, inc=1, device_id=(pair, me), device_id_type=MESH)
         pass_on(1)
         to_vmem.wait()
         own[0].wait()
@@ -204,9 +204,9 @@
         length = lengths[0, 0]
         valid = lax.broadcasted_iota(jnp.int32, (tok, 2 * span), 1) < length
         low = lax.broadcasted_iota(jnp.int32, (tok, 2 * head_dim), 1) < head_dim
-        mask_low = jnp.where(low, 1.0, 0.0).astype(BF16)
-        mask_high = jnp.where(low, 0.0, 1.0).astype(BF16)
         scale = 1.0 / (head_dim ** 0.5)
+        mask_low = jnp.where(low, scale, 0.0).astype(BF16)
+        mask_high = jnp.where(low, 0.0, scale).astype(BF16)
 
         @pl.loop(0, HEADS // 2)
         def _(i):
@@ -216,11 +216,11 @@
             for mask in (mask_low, mask_high):
                 scores = lax.dot_general(
                     q2 * mask, k2, (((1,), (1,)), ((), ())), preferred_element_type=F32
-                ) * scale
+                )
                 scores = jnp.where(valid, scores, -1e30)
                 scores = scores - jnp.max(scores, axis=-1, keepdims=True)
                 weights = jnp.exp(scores)
-                probs = (weights / jnp.sum(weights, axis=-1, keepdims=True)).astype(BF16)
+                probs = (weights * (1.0 / jnp.sum(weights, axis=-1, keepdims=True))).astype(BF16)
                 parts.append(jnp.dot(probs, v2, preferred_element_type=F32))
             cbuf[:, cols] = jnp.where(low, parts[0], parts[1]).astype(BF16)
 

time: 83 us -> 88.5 us (1.066)
  the two profiles are of different devices: /device:TPU:7 before, /device:TPU:15 now
where the time goes in v5:
time: 88.5 us; the launch traced here: 88.3 us
  Pallas kernels  85 us (96%)
  local copies, waits for them, and re-layouts  2.02 us (2%)
  between operations  1.3 us (1%)
    pallas_call x1, Pallas kernels, shards(): pl.pallas_call(functools.partial(relay, sections, experts, cap), out_shap...  85 us
    unnamed x1, local copies, waits for them, and re-layouts  2.02 us

profile of v5, /device:TPU:15, one launch (start us, length us, event | category | flops | bytes accessed | tf_op | source)
XLA Modules:
  0.0 88.3 jit_solution(10740873314690317905)
XLA Ops:
  1.3 85.0 %shard_map.100 = bf16[1,256,1408]{2,1,0:T(8,128)(2,1)} custom-call(bf16[1,256,1024]{2,1,0:T(8,128)(2,1)} %tokens.1, f32[1,256]{1,0:T(1,128)} %gates.1, s32[1,256]{1,0:T(1,128)} %bitcast.1, s32[1,1]{1,0:T(1,128)S(6)} %copy.12.capacity, s32[1,1]{1,0:T(1,128)S(6)} %copy.13.lengths, bf16[1,128,1024]{2,1,0:T(8,128)(2,1)} %mem_k.1, bf16[1,128,1024]{2,1,0:T(8,128)(2,1)} %mem_v.1, ...), custom_call_target="tpu_custom_call" | custom-call | flops 2550136832 | bytes 11272192 | tf_op jit(solution)/shard_map/pallas_call | solution.py:380
  86.3 2.0 %copy.14 = bf16[1,256,1408]{2,1,0:T(8,128)(2,1)} copy(bf16[1,256,1408]{2,1,0:T(8,128)(2,1)} %shard_map.100) | data formatting | bytes 1441792
